TPU v7x, 32 devices: a whole 2x2x4 slice. The times are simulated.
32 devices in a mesh: frame: 2 (over y), row: 4 (over x, core), fsdp: 4 (over z).
Axes of the slice: x: 2, y: 2, z: 4, core: 2. Of those that a mesh axis runs over, the one named last changes fastest.
Arguments:
- query: bfloat16 [4, 16, 48, 2560], P('frame', 'row', 'fsdp'), may hold values from -20 to 20
- key_value: bfloat16 [2, 4, 16, 48, 2560], P(None, 'frame', 'row', 'fsdp'), may hold values from -6 to 6
- out_weight: bfloat16 [2560, 2560], P(None, 'fsdp'), may hold values from -0.125 to 0.125
- mod_table: float32 [16, 2560], replicated, may hold values from -4 to 4
- step: int32 [1], replicated, may hold values from 0 to 15
- window: int32 [20, 3], replicated, may hold values from 0 to 2, as said below
Outputs:
- mixed: bfloat16 [4, 16, 48, 2560], P('frame', 'row', 'fsdp')
Inputs may be any that keep to these rules, and one draw needn't show every extreme that they name: `window`: Half-extents along frames are at most 1, along rows at most 2, along columns at most 2; every head has a nonzero half-extent along some dimension; some head has exactly 1, 2 and 2, and some head has 0 along frames.
All inputs are finite; a program needn't handle non-finite values.
Results may differ from a plain program's by a relative error of at most 0.0057.
Values may be sent and summed in bfloat16 or wider, within the bound.
A program may use at most 128 MiB of HBM per device.

v0:
```python
import math

import jax
import jax.numpy as jnp
from jax import lax
from jax.sharding import PartitionSpec as P

HEAD_DIM = 128
WF = 1
WR = 2
WC = 2


def with_halo(cells, sides, width):
    for axis, dim in sides:
        count = lax.axis_size(axis)
        ends = count - 1
        head = lax.slice_in_dim(cells, 0, width, axis=dim)
        tail = lax.slice_in_dim(cells, cells.shape[dim] - width, cells.shape[dim], axis=dim)
        cells = jnp.concatenate(
            [
                lax.ppermute(tail, axis, [(i, (i + 1) % count) for i in range(ends)]),
                cells,
                lax.ppermute(head, axis, [((i + 1) % count, i) for i in range(ends)]),
            ],
            axis=dim,
        )
    return cells


def axis_allowed(shard, reach, position, axis_count, extents):
    own_pos = jnp.arange(shard)
    margin_pos = jnp.arange(shard + 2 * reach)
    offset = margin_pos[None, :] - reach - own_pos[:, None]
    first_cell = position * shard
    whole_count = shard * axis_count
    global_pos = first_cell + margin_pos - reach
    inside = (global_pos >= 0) & (global_pos < whole_count)
    return (jnp.abs(offset)[None, :, :] <= extents[:, None, None]) & inside[None, None, :]


def body(query, key_value, out_weight, mod_table, step, window):
    frame_count, row_count, column_count, feature_width = query.shape
    head_count = feature_width // HEAD_DIM
    tokens = frame_count * row_count * column_count
    padded = with_halo(key_value, (("frame", 1),), WF)
    padded = with_halo(padded, (("row", 2), ("fsdp", 3)), WR)
    key_rows = padded[0].reshape(-1, head_count, HEAD_DIM)
    value_rows = padded[1].reshape(-1, head_count, HEAD_DIM)
    queries = query.reshape(tokens, head_count, HEAD_DIM)
    scores = jnp.einsum("qhd,khd->hqk", queries, key_rows, preferred_element_type=jnp.float32)
    scores = scores * (1.0 / math.sqrt(HEAD_DIM))
    frame_ok = axis_allowed(
        frame_count, WF, lax.axis_index("frame"), lax.axis_size("frame"), window[:, 0]
    )
    row_ok = axis_allowed(row_count, WR, lax.axis_index("row"), lax.axis_size("row"), window[:, 1])
    column_ok = axis_allowed(
        column_count, WC, lax.axis_index("fsdp"), lax.axis_size("fsdp"), window[:, 2]
    )
    allowed = (
        frame_ok[:, :, None, None, :, None, None]
        & row_ok[:, None, :, None, None, :, None]
        & column_ok[:, None, None, :, None, None, :]
    )
    allowed = allowed.reshape(head_count, tokens, key_rows.shape[0])
    scores = jnp.where(allowed, scores, jnp.float32(-1e30))
    highest = jnp.max(scores, axis=-1, keepdims=True)
    exponent = jnp.exp(scores - highest)
    denominator = jnp.sum(exponent, axis=-1, keepdims=True)
    weights = (exponent / denominator).astype(jnp.bfloat16)
    attn = jnp.einsum("hqk,khd->qhd", weights, value_rows, preferred_element_type=jnp.float32)
    attn = attn.astype(jnp.bfloat16).reshape(tokens, feature_width)
    gate = lax.dynamic_slice_in_dim(mod_table, step[0], 1, 0)[0]
    mixed = (
        jnp.dot(
            attn,
            lax.all_gather(out_weight, "fsdp", axis=1, tiled=True),
            preferred_element_type=jnp.float32,
        )
        * gate
    ).astype(jnp.bfloat16)
    return mixed.reshape(frame_count, row_count, column_count, -1)


def solution(mesh):
    return jax.shard_map(
        body,
        mesh=mesh,
        in_specs=(
            P("frame", "row", "fsdp", None),
            P(None, "frame", "row", "fsdp", None),
            P(None, "fsdp"),
            P(),
            P(),
            P(),
        ),
        out_specs=P("frame", "row", "fsdp", None),
        check_vma=False,
    )
```

profile of v0, /device:TPU:1, one launch (start us, length us, event | category | flops | bytes accessed | tf_op | source)
XLA Modules:
  0.0 267.2 jit_solution(351044591674200779)
XLA Ops:
  6.5 0.0 all-gather.2.cloned.1.call-start
  6.5 0.7 all-gather.2.cloned.1.call-update
  7.3 0.5 copy-done.5
  7.8 0.3 fusion.27
  8.1 0.1 copy.54
  8.2 4.8 %collective-permute-start = (bf16[2,1,4,12,2560]{4,3,2,1,0:T(8,128)(2,1)S(1)}, bf16[2,1,4,12,2560]{4,3,2,1,0:T(8,128)(2,1)}, u32[]{:S(2)}, u32[]{:S(2)}) collective-permute-start(bf16[2,1,4,12,2560]{4,3,2,1,0:T(8,128)(2,1)S(1)} %copy.54), channel_id=1, source_target_pairs={{0,16},{1,17},{2,18},{3,19},{4,20},{5,21},{6,22},{7,23},{8,24},{9,... | collective-permute-start | bytes 1474568 | tf_op jit(solution)/shard_map/ppermute | solution.py:22
  13.1 0.1 copy.55
  13.2 1.3 collective-permute-start.1
  14.6 11.0 %collective-permute-done = bf16[2,1,4,12,2560]{4,3,2,1,0:T(8,128)(2,1)} collective-permute-done((bf16[2,1,4,12,2560]{4,3,2,1,0:T(8,128)(2,1)S(1)}, bf16[2,1,4,12,2560]{4,3,2,1,0:T(8,128)(2,1)}, u32[]{:S(2)}, u32[]{:S(2)}) %collective-permute-start) | collective-permute-done | bytes 491552 | tf_op jit(solution)/shard_map/ppermute | solution.py:22
  25.6 1.2 constant_dynamic-update-slice_fusion.1
  26.8 1.5 copy_dynamic-update-slice_fusion
  28.3 2.1 collective-permute-done.1
  30.4 1.1 constant_dynamic-update-slice_fusion
  31.6 0.2 fusion.26
  31.7 4.9 %collective-permute-start.2 = (bf16[2,4,2,12,2560]{4,3,2,1,0:T(8,128)(2,1)S(1)}, bf16[2,4,2,12,2560]{4,3,2,1,0:T(8,128)(2,1)S(1)}, u32[]{:S(2)}, u32[]{:S(2)}) collective-permute-start(bf16[2,4,2,12,2560]{4,3,2,1,0:T(8,128)(2,1)S(1)} %get-tuple-element.9), channel_id=1, source_target_pairs={{0,4},{4,8},{8,12},{1,5},{5,9},{9,13},{2,6},{6,10},{10,14},{3,7},{... | collective-permute-start | bytes 2949128 | tf_op jit(solution)/shard_map/ppermute | solution.py:22
  36.6 1.9 collective-permute-start.3
  38.6 0.1 compare_and_fusion.2
  38.7 0.1 compare_and_fusion.1
  38.8 0.1 compare_and_fusion
  38.9 0.2 broadcast_and_fusion.1
  39.0 12.1 %collective-permute-done.2 = bf16[2,4,2,12,2560]{4,3,2,1,0:T(8,128)(2,1)S(1)} collective-permute-done((bf16[2,4,2,12,2560]{4,3,2,1,0:T(8,128)(2,1)S(1)}, bf16[2,4,2,12,2560]{4,3,2,1,0:T(8,128)(2,1)S(1)}, u32[]{:S(2)}, u32[]{:S(2)}) %collective-permute-start.2) | collective-permute-done | bytes 983072 | tf_op jit(solution)/shard_map/ppermute | solution.py:22
  51.2 4.8 %collective-permute-done.3 = bf16[2,4,2,12,2560]{4,3,2,1,0:T(8,128)(2,1)S(1)} collective-permute-done((bf16[2,4,2,12,2560]{4,3,2,1,0:T(8,128)(2,1)S(1)}, bf16[2,4,2,12,2560]{4,3,2,1,0:T(8,128)(2,1)S(1)}, u32[]{:S(2)}, u32[]{:S(2)}) %collective-permute-start.3) | collective-permute-done | bytes 983072 | tf_op jit(solution)/shard_map/ppermute | solution.py:24
  56.0 1.4 pad_maximum_fusion.3
  57.4 0.9 copy.28
  58.3 4.0 %collective-permute-start.4 = (bf16[2,4,8,2,2560]{4,2,3,1,0:T(8,128)(2,1)}, bf16[2,4,8,2,2560]{4,2,3,1,0:T(8,128)(2,1)}, u32[]{:S(2)}, u32[]{:S(2)}) collective-permute-start(bf16[2,4,8,2,2560]{4,2,3,1,0:T(8,128)(2,1)} %copy.28), channel_id=1, source_target_pairs={{0,1},{1,2},{2,3},{4,5},{5,6},{6,7},{8,9},{9,10},{10,11},{12,13},{... | collective-permute-start | bytes 1966088 | tf_op jit(solution)/shard_map/ppermute | solution.py:22
  62.3 1.0 copy.29
  63.3 1.4 collective-permute-start.5
  64.7 6.6 %broadcast_and_fusion = pred[20,2,4,12,4,8,16]{6,5,4,3,2,1,0:T(8,128)(4,1)} fusion(pred[20,12,16]{2,1,0:T(8,128)(4,1)S(1)} %compare_and_fusion, pred[20,2,4,4,8]{4,3,2,1,0:T(4,128)(4,1)S(1)} %broadcast_and_fusion.1), kind=kLoop, calls=%fused_computation.1 | loop fusion | flops 983040 | bytes 992000 | tf_op jit(solution)/shard_map/and | solution.py:61
  71.3 0.1 copy.32
  71.4 1.2 reshape.132
  72.6 18.0 %and.110 = pred[20,96,512]{2,1,0:T(32,128)(4,1)} reshape(pred[20,2,4,12,4,8,16]{6,5,4,3,2,1,0:T(8,128)(4,1)} %broadcast_and_fusion) | data formatting | bytes 1966080 | tf_op jit(solution)/shard_map/and | solution.py:61
  91.4 0.0 collective-permute-done.4
  91.4 1.6 copy.30
  93.0 19.1 %collective-permute-done.5 = bf16[2,4,8,2,2560]{4,2,3,1,0:T(8,128)(2,1)} collective-permute-done((bf16[2,4,8,2,2560]{4,2,3,1,0:T(8,128)(2,1)}, bf16[2,4,8,2,2560]{4,2,3,1,0:T(8,128)(2,1)}, u32[]{:S(2)}, u32[]{:S(2)}) %collective-permute-start.5) | collective-permute-done | bytes 655392 | tf_op jit(solution)/shard_map/ppermute | solution.py:24
  112.1 1.6 copy.31
  113.8 6.0 %pad_maximum_fusion = bf16[2,4,8,16,2560]{4,3,2,1,0:T(8,128)(2,1)S(1)} fusion(bf16[2,4,8,2,2560]{4,3,2,1,0:T(2,128)(2,1)S(1)} %copy.31, bf16[2,4,2,12,2560]{4,3,2,1,0:T(8,128)(2,1)} %copy-done.3, bf16[2,4,4,12,2560]{4,3,2,1,0:T(8,128)(2,1)S(1)} %constant_dynamic-update-slice_fusion, bf16[2,4,2,12,2560]{4,3,2,1,0:T(8,128)(2,1)} %copy-done.2, ...), kind=kLoop, calls=%fused_computation.2 | loop fusion | flops 26214400 | bytes 10485760 | tf_op jit(solution)/shard_map/concatenate | solution.py:20
  119.7 2.7 fusion.25
  122.4 4.2 %reshape_squeeze.7 = bf16[512,20,128]{2,1,0:T(8,128)(2,1)S(1)} reshape(bf16[1,4,8,16,2560]{4,3,2,1,0:T(8,128)(2,1)} %get-tuple-element.5) | data formatting | bytes 5242880 | tf_op jit(solution)/shard_map/reshape;squeeze | solution.py:48
  126.6 5.5 %reshape_squeeze.6 = bf16[512,20,128]{2,1,0:T(8,128)(2,1)} reshape(bf16[1,4,8,16,2560]{4,3,2,1,0:T(8,128)(2,1)} %get-tuple-element.6) | data formatting | bytes 5242880 | tf_op jit(solution)/shard_map/reshape;squeeze | solution.py:49
  132.1 2.2 fusion.4
  134.3 1.9 copy-done.4
  136.2 1.4 fusion.28
  137.6 0.5 copy-done.6
  138.1 6.8 %fusion.12 = bf16[20,12,8,128]{3,2,1,0:T(8,128)(2,1)} fusion(bf16[512,20,128]{2,1,0:T(8,128)(2,1)S(1)} %copy-done.6, f32[20,96]{1,0:T(8,128)S(1)} %fusion.28, pred[20,96,512]{2,1,0:T(32,128)(4,1)} %and.110, f32[20,512,96]{1,2,0:T(8,128)} %copy-done.4), kind=kOutput, calls=%fused_computation.16 | convolution fusion | flops 256821632 | bytes 8035840 | tf_op jit(solution)/shard_map/hqk,khd->qhd/dot_general | solution.py:71
  144.9 107.1 %all-gather.2.cloned.1.call-done = bf16[2560,2560]{1,0:T(8,128)(2,1)} async-done(((bf16[2560,640]{1,0:T(8,128)(2,1)}), bf16[2560,2560]{1,0:T(8,128)(2,1)}) %all-gather.2.cloned.1.call-update) | async-done | bytes 13107216 | tf_op jit(solution)/shard_map/all_gather | solution.py:77
  252.0 7.1 %fusion.1 = bf16[96,2560]{1,0:T(8,128)(2,1)S(1)} fusion(bf16[2560,2560]{1,0:T(8,128)(2,1)} %all-gather.2.cloned.1.call-done, bf16[20,12,8,128]{3,2,1,0:T(8,128)(2,1)} %fusion.12, f32[2560]{0:T(1024)S(1)} %dynamic-slice_reduce_fusion), kind=kOutput, calls=%fused_computation.7 | convolution fusion | flops 1258782720 | bytes 14100480 | tf_op jit(solution)/shard_map/dot_general | solution.py:75
  259.1 0.1 reshape.134
  259.2 1.2 copy.37
  (28 shorter events, 0.1 us)
Async XLA Ops:
  6.5 84.8 %copy-start = (f32[16,2560]{1,0:T(8,128)S(1)}, f32[16,2560]{1,0:T(8,128)}, u32[]{:S(2)}) copy-start(f32[16,2560]{1,0:T(8,128)} %param.9) | copy-start | bytes 491524
  6.5 1.2 copy-start.5
  6.5 8.0 %copy-start.9 = (s32[20,3]{0,1:T(4,128)S(1)}, s32[20,3]{0,1:T(4,128)}, u32[]{:S(2)}) copy-start(s32[20,3]{0,1:T(4,128)} %param.11) | copy-start | bytes 724
  6.5 245.4 %all-gather.2.cloned.1.call-start = ((), (), s32[]{:S(2)}) async-start(), calls=%async_computation | async-start | bytes 16384000 | tf_op jit(solution)/shard_map/all_gather | solution.py:77
  8.2 17.4 %collective-permute-start = (bf16[2,1,4,12,2560]{4,3,2,1,0:T(8,128)(2,1)S(1)}, bf16[2,1,4,12,2560]{4,3,2,1,0:T(8,128)(2,1)}, u32[]{:S(2)}, u32[]{:S(2)}) collective-permute-start(bf16[2,1,4,12,2560]{4,3,2,1,0:T(8,128)(2,1)S(1)} %copy.54), channel_id=1, source_target_pairs={{0,16},{1,17},{2,18},{3,19},{4,20},{5,21},{6,22},{7,23},{8,24},{9,... | collective-permute-start | bytes 1474568 | tf_op jit(solution)/shard_map/ppermute | solution.py:22
  13.2 17.3 %collective-permute-start.1 = (bf16[2,1,4,12,2560]{4,3,2,1,0:T(8,128)(2,1)S(1)}, bf16[2,1,4,12,2560]{4,3,2,1,0:T(8,128)(2,1)}, u32[]{:S(2)}, u32[]{:S(2)}) collective-permute-start(bf16[2,1,4,12,2560]{4,3,2,1,0:T(8,128)(2,1)S(1)} %copy.55), channel_id=1, source_target_pairs={{16,0},{17,1},{18,2},{19,3},{20,4},{21,5},{22,6},{23,7},{24,8},{25... | collective-permute-start | bytes 1474568 | tf_op jit(solution)/shard_map/ppermute | solution.py:24
  31.7 19.4 %collective-permute-start.2 = (bf16[2,4,2,12,2560]{4,3,2,1,0:T(8,128)(2,1)S(1)}, bf16[2,4,2,12,2560]{4,3,2,1,0:T(8,128)(2,1)S(1)}, u32[]{:S(2)}, u32[]{:S(2)}) collective-permute-start(bf16[2,4,2,12,2560]{4,3,2,1,0:T(8,128)(2,1)S(1)} %get-tuple-element.9), channel_id=1, source_target_pairs={{0,4},{4,8},{8,12},{1,5},{5,9},{9,13},{2,6},{6,10},{10,14},{3,7},{... | collective-permute-start | bytes 2949128 | tf_op jit(solution)/shard_map/ppermute | solution.py:22
  36.6 19.3 %collective-permute-start.3 = (bf16[2,4,2,12,2560]{4,3,2,1,0:T(8,128)(2,1)S(1)}, bf16[2,4,2,12,2560]{4,3,2,1,0:T(8,128)(2,1)S(1)}, u32[]{:S(2)}, u32[]{:S(2)}) collective-permute-start(bf16[2,4,2,12,2560]{4,3,2,1,0:T(8,128)(2,1)S(1)} %get-tuple-element.10), channel_id=1, source_target_pairs={{4,0},{8,4},{12,8},{5,1},{9,5},{13,9},{6,2},{10,6},{14,10},{7,3},{... | collective-permute-start | bytes 2949128 | tf_op jit(solution)/shard_map/ppermute | solution.py:24
  51.2 7.1 %copy-start.2 = (bf16[2,4,2,12,2560]{4,3,2,1,0:T(8,128)(2,1)}, bf16[2,4,2,12,2560]{4,3,2,1,0:T(8,128)(2,1)S(1)}, u32[]{:S(2)}) copy-start(bf16[2,4,2,12,2560]{4,3,2,1,0:T(8,128)(2,1)S(1)} %collective-permute-done.2) | copy-start | bytes 2949124
  56.0 2.3 copy-start.3
  58.3 33.1 %collective-permute-start.4 = (bf16[2,4,8,2,2560]{4,2,3,1,0:T(8,128)(2,1)}, bf16[2,4,8,2,2560]{4,2,3,1,0:T(8,128)(2,1)}, u32[]{:S(2)}, u32[]{:S(2)}) collective-permute-start(bf16[2,4,8,2,2560]{4,2,3,1,0:T(8,128)(2,1)} %copy.28), channel_id=1, source_target_pairs={{0,1},{1,2},{2,3},{4,5},{5,6},{6,7},{8,9},{9,10},{10,11},{12,13},{... | collective-permute-start | bytes 1966088 | tf_op jit(solution)/shard_map/ppermute | solution.py:22
  63.3 8.0 %copy-start.8 = (bf16[2,4,12,2560]{3,1,2,0:T(4,128)(2,1)S(1)}, bf16[2,4,12,2560]{3,1,2,0:T(4,128)(2,1)}, u32[]{:S(2)}) copy-start(bf16[2,4,12,2560]{3,1,2,0:T(4,128)(2,1)} %param.6) | copy-start | bytes 1474564
  63.3 48.8 %collective-permute-start.5 = (bf16[2,4,8,2,2560]{4,2,3,1,0:T(8,128)(2,1)}, bf16[2,4,8,2,2560]{4,2,3,1,0:T(8,128)(2,1)}, u32[]{:S(2)}, u32[]{:S(2)}) collective-permute-start(bf16[2,4,8,2,2560]{4,2,3,1,0:T(8,128)(2,1)} %copy.29), channel_id=1, source_target_pairs={{1,0},{2,1},{3,2},{5,4},{6,5},{7,6},{9,8},{10,9},{11,10},{13,12},{... | collective-permute-start | bytes 1966088 | tf_op jit(solution)/shard_map/ppermute | solution.py:24
  132.1 4.0 %copy-start.7 = (pred[20,96,512]{2,1,0:T(32,128)(4,1)S(1)}, pred[20,96,512]{2,1,0:T(32,128)(4,1)}, u32[]{:S(2)}) copy-start(pred[20,96,512]{2,1,0:T(32,128)(4,1)} %and.110) | copy-start | bytes 2949124
  134.3 1.9 copy-start.4
  136.2 1.9 copy-start.6
  252.0 8.4 %copy-start.1 = (f32[16,2560]{1,0:T(8,128)S(1)}, f32[16,2560]{1,0:T(8,128)}, u32[]{:S(2)}) copy-start(f32[16,2560]{1,0:T(8,128)} %param.9) | copy-start | bytes 491524
Sparse Core Ops, SparseCore 0:
  8.9 242.9 all-gather.1
where the time goes:
time: 269 us; the launch traced here: 267 us
  waiting for transfers between devices  157 us (58%)
  local copies, waits for them, and re-layouts  45.6 us (17%)
  starting transfers between devices  18.4 us (7%)
  matrix products  16.1 us (6%)
  other arithmetic  15.9 us (6%)
  between operations  14.3 us (5%)
    all_gather x1, waiting for transfers between devices, body(): lax.all_gather(out_weight, 'fsdp', axis=1, tiled=True)  107 us
    ppermute x3, waiting for transfers between devices, with_halo(): lax.ppermute(head, axis, [((i + 1) % count, i) for i in range(ends)])  26 us
    ppermute x3, waiting for transfers between devices, with_halo(): lax.ppermute(tail, axis, [(i, (i + 1) % count) for i in range(ends)])  23.1 us
    and x1, local copies, waits for them, and re-layouts, body(): frame_ok[:, :, None, None, :, None, None]  18 us
    ppermute x3, starting transfers between devices, with_halo(): lax.ppermute(tail, axis, [(i, (i + 1) % count) for i in range(ends)])  13.7 us
    dot_general x1, matrix products, body(): jnp.dot(attn, lax.all_gather(out_weight, 'fsdp', axis=1, tiled=True), pre...  7.13 us
    dot_general x1, matrix products, body(): jnp.einsum('hqk,khd->qhd', weights, value_rows, preferred_element_type=jn...  6.79 us
    and x2, other arithmetic, body(): frame_ok[:, :, None, None, :, None, None]  6.74 us
  transfers between devices with their start and end apart: 7, of which 6 were waited for; matrix products, arithmetic and copies ran while one was open for 25% of the time, Pallas kernels for 0%

commit v1 on v0

v1 whole, which is shorter than its diff:
```python
import functools
import math

import jax
import jax.numpy as jnp
from jax import lax
from jax.experimental import pallas as pl
from jax.experimental.pallas import tpu as pltpu
from jax.sharding import PartitionSpec as P

HEAD_DIM = 128
QUARTERS = 4
MESH = pl.DeviceIdType.MESH


def kernel(
    sizes, gin, q_ref, w_hbm, gate_ref, win_ref, out_ref,
    grid, bias, attn, w_ref, y_out, y_in,
    halo_send, halo_recv, attn_send, attn_recv, y_send, y_recv, local_sem,
):
    n_frame, n_row, n_col = sizes
    slots = grid.shape[0]
    groups = attn.shape[0]
    tokens = attn.shape[2]
    own_frames, own_rps, own_cps = gin.shape[:3]
    me_f = lax.axis_index("frame")
    me_r = lax.axis_index("row")
    me_c = lax.axis_index("fsdp")

    w_copy = pltpu.make_async_copy(w_hbm, w_ref, local_sem.at[0])
    w_copy.start()
    own_copy = pltpu.make_async_copy(
        gin, grid.at[pl.ds(0, own_frames), pl.ds(0, own_rps), pl.ds(0, own_cps)], local_sem.at[1]
    )
    own_copy.start()

    barrier = pltpu.get_barrier_semaphore()

    def neighbours(axis, me, count):
        return ((axis, me + 1, me < count - 1), (axis, me - 1, me > 0))

    near = neighbours("frame", me_f, n_frame) + neighbours("row", me_r, n_row)
    for axis, other, there in near:
        @pl.when(there)
        def _():
            pl.semaphore_signal(barrier, inc=1, device_id={axis: other}, device_id_type=MESH)

    def greet(k, carry):
        peer = lax.rem(me_c + k, n_col)
        pl.semaphore_signal(barrier, inc=1, device_id={"fsdp": peer}, device_id_type=MESH)
        return carry

    lax.fori_loop(1, n_col, greet, 0)
    greetings = n_col - 1
    for _, _, there in near:
        greetings += there.astype(jnp.int32)
    pl.semaphore_wait(barrier, greetings)

    def copy(src, dst, index, axis, other):
        return pltpu.make_async_remote_copy(
            src_ref=src, dst_ref=dst, send_sem=halo_send.at[index], recv_sem=halo_recv.at[index],
            device_id={axis: other}, device_id_type=MESH,
        )

    own_f = pl.ds(0, own_frames)
    halo_f = pl.ds(own_frames, slots - own_frames)
    own_r = pl.ds(0, own_rps)
    halo_r = pl.ds(own_rps, 2)
    own_c = pl.ds(0, own_cps)
    below, above = own_rps, own_rps + 1
    left, right = own_cps, own_cps + 1
    low_slot, high_slot = own_frames, slots - 1
    steps = {}

    def add(name, axis, me, count, index, up, down):
        steps[name] = (
            (copy(up[0], up[1], index, axis, me + 1), me < count - 1, me > 0),
            (copy(down[0], down[1], index + 1, axis, me - 1), me > 0, me < count - 1),
        )

    add("f", "frame", me_f, n_frame, 0,
        (gin.at[own_frames - 1], grid.at[low_slot, own_r, own_c]),
        (gin.at[0], grid.at[high_slot, own_r, own_c]))
    add("r1", "row", me_r, n_row, 2,
        (gin.at[:, own_rps - 1], grid.at[own_f, below, own_c]),
        (gin.at[:, 0], grid.at[own_f, above, own_c]))
    add("r2", "row", me_r, n_row, 4,
        (grid.at[halo_f, own_rps - 1, own_c], grid.at[halo_f, below, own_c]),
        (grid.at[halo_f, 0, own_c], grid.at[halo_f, above, own_c]))
    add("c1", "fsdp", me_c, n_col, 6,
        (gin.at[:, :, own_cps - 1], grid.at[own_f, own_r, left]),
        (gin.at[:, :, 0], grid.at[own_f, own_r, right]))
    add("c2", "fsdp", me_c, n_col, 8,
        (grid.at[own_f, halo_r, own_cps - 1], grid.at[own_f, halo_r, left]),
        (grid.at[own_f, halo_r, 0], grid.at[own_f, halo_r, right]))
    all_r = pl.ds(0, own_rps + 2)
    add("c3", "fsdp", me_c, n_col, 10,
        (grid.at[halo_f, all_r, own_cps - 1], grid.at[halo_f, all_r, left]),
        (grid.at[halo_f, all_r, 0], grid.at[halo_f, all_r, right]))

    def start(name):
        for step, sends, _ in steps[name]:
            @pl.when(sends)
            def _():
                step.start()

    def arrive(name):
        for step, _, receives in steps[name]:
            @pl.when(receives)
            def _():
                step.wait_recv()

    start("f")
    start("r1")
    start("c1")

    for edge, at_edge in (
        ((slice(None), below), me_r == 0),
        ((slice(None), above), me_r == n_row - 1),
    ):
        @pl.when(at_edge)
        def _():
            for slot in range(slots):
                grid[(slot, edge[1], pl.ds(0, own_cps))] = jnp.zeros(
                    (own_cps,) + grid.shape[3:], grid.dtype)
    for place, at_edge in ((left, me_c == 0), (right, me_c == n_col - 1)):
        @pl.when(at_edge)
        def _():
            for slot in range(slots):
                grid[slot, :, place] = jnp.zeros((grid.shape[1],) + grid.shape[3:], grid.dtype)
    if slots - own_frames == 2:
        for place, at_edge in ((low_slot, me_f == 0), (high_slot, me_f == n_frame - 1)):
            @pl.when(at_edge)
            def _():
                for pair in range(own_rps):
                    grid[place, pair, pl.ds(0, own_cps)] = jnp.zeros(
                        (own_cps,) + grid.shape[3:], grid.dtype)

    arrive("r1")
    start("c2")

    keys = bias.shape[2]
    shape = (tokens, keys)
    rows, columns = 2 * own_rps, 2 * own_cps
    at = lax.broadcasted_iota(jnp.int32, shape, 0)
    q_f = jnp.zeros(shape, jnp.int32)
    for f in range(1, own_frames):
        q_f += (at >= f * rows * columns).astype(jnp.int32)
    at = at - q_f * (rows * columns)
    q_r = jnp.zeros(shape, jnp.int32)
    for r in range(1, rows):
        q_r += (at >= r * columns).astype(jnp.int32)
    q_c = at - q_r * columns
    lane = lax.broadcasted_iota(jnp.int32, shape, 1)
    slot = lane >> 7
    pair_r = (lane >> 5) & 3
    pair_c = (lane >> 2) & 7
    if slots - own_frames == 1:
        halo_at = jnp.where(me_f == 0, own_frames, -1)
        k_f = jnp.where(slot == own_frames, halo_at, slot)
    else:
        k_f = jnp.where(slot == low_slot, -1, slot)
        k_f = jnp.where(slot == high_slot, own_frames, k_f)
    pair_r = jnp.where(pair_r == below, -1, jnp.where(pair_r == above, own_rps, pair_r))
    pair_c = jnp.where(pair_c == left, -1, jnp.where(pair_c == right, own_cps, pair_c))
    k_r = 2 * pair_r + ((lane >> 1) & 1)
    k_c = 2 * pair_c + (lane & 1)
    g_f = k_f + me_f * own_frames
    g_r = k_r + me_r * rows
    g_c = k_c + me_c * columns
    inside = (
        (g_f >= 0) & (g_f < n_frame * own_frames)
        & (g_r >= 0) & (g_r < n_row * rows)
        & (g_c >= 0) & (g_c < n_col * columns)
    )
    d_f = jnp.where(inside, jnp.abs(k_f - q_f), 1000)
    d_r = jnp.abs(k_r - q_r)
    d_c = jnp.abs(k_c - q_c)

    def make_bias(head, carry):
        ok = (d_f <= win_ref[head, 0]) & (d_r <= win_ref[head, 1]) & (d_c <= win_ref[head, 2])
        bias[head] = jnp.where(ok, jnp.float32(0), jnp.float32(-1e30))
        return carry

    lax.fori_loop(0, QUARTERS * groups, make_bias, 0)

    arrive("f")
    start("r2")
    arrive("r2")
    start("c3")
    own_copy.wait()
    arrive("c1")
    arrive("c2")
    arrive("c3")

    granules = slots * grid.shape[1] * grid.shape[2]
    scale = 1.0 / math.sqrt(HEAD_DIM)

    def attn_copy(j, k):
        peer = lax.rem(me_c + k, n_col)
        return pltpu.make_async_remote_copy(
            src_ref=attn.at[j, me_c], dst_ref=attn.at[j, me_c],
            send_sem=attn_send.at[j, k], recv_sem=attn_recv.at[j, k],
            device_id={"fsdp": peer}, device_id_type=MESH,
        )

    def attn_arrival(j, k):
        peer = lax.rem(me_c - k + n_col, n_col)
        return pltpu.make_async_remote_copy(
            src_ref=attn.at[j, me_c], dst_ref=attn.at[j, peer],
            send_sem=attn_send.at[j, k], recv_sem=attn_recv.at[j, k],
            device_id={"fsdp": peer}, device_id_type=MESH,
        )

    for j in range(groups):
        lanes = pl.ds(j * 2 * HEAD_DIM, 2 * HEAD_DIM)
        block = grid[:, :, :, :, lanes].astype(jnp.float32)
        block = block.reshape(granules // 2, 2, 2, 8, 2 * HEAD_DIM)
        first, second = block[:, 0], block[:, 1]
        flat = (granules // 2 * 2 * 8, 2 * HEAD_DIM)
        turned_first = pltpu.roll(block[:, 0].reshape(-1, 8, 2 * HEAD_DIM), 4, 1).reshape(first.shape)
        turned_second = pltpu.roll(block[:, 1].reshape(-1, 8, 2 * HEAD_DIM), 4, 1).reshape(first.shape)
        upper = lax.broadcasted_iota(jnp.int32, first.shape, 2) < 4
        even = jnp.where(upper, first, turned_second)
        odd = jnp.where(upper, turned_first, second)
        for quarter in range(QUARTERS):
            head = quarter * groups + j
            dense = (even, odd)[quarter % 2][:, quarter // 2].reshape(keys, 2 * HEAD_DIM)
            dense = dense.astype(jnp.bfloat16)
            query = q_ref[:, pl.ds(head * HEAD_DIM, HEAD_DIM)]
            scores = lax.dot_general(
                query, dense[:, :HEAD_DIM], (((1,), (1,)), ((), ())),
                preferred_element_type=jnp.float32,
            )
            scores = scores * scale + bias[head]
            exponent = jnp.exp(scores - jnp.max(scores, axis=-1, keepdims=True))
            denominator = jnp.sum(exponent, axis=-1, keepdims=True)
            weights = (exponent * (1.0 / denominator)).astype(jnp.bfloat16)
            result = jnp.dot(weights, dense[:, HEAD_DIM:], preferred_element_type=jnp.float32)
            attn[j, me_c, :, pl.ds(quarter * HEAD_DIM, HEAD_DIM)] = result.astype(jnp.bfloat16)

        def send(k, carry):
            attn_copy(j, k).start()
            return carry

        lax.fori_loop(1, n_col, send, 0)

    w_copy.wait()
    total = None
    width = w_ref.shape[1]
    for j in range(groups):
        def gather(k, carry):
            attn_arrival(j, k).wait_recv()
            return carry

        lax.fori_loop(1, n_col, gather, 0)
        weight = jnp.concatenate(
            [w_ref[pl.ds((quarter * groups + j) * HEAD_DIM, HEAD_DIM), :] for quarter in range(QUARTERS)],
            axis=0,
        )
        part = jnp.dot(
            attn[j].reshape(n_col * tokens, QUARTERS * HEAD_DIM), weight,
            preferred_element_type=jnp.float32,
        )
        total = part if total is None else total + part
    y_out[...] = (total * gate_ref[...]).astype(jnp.bfloat16).reshape(n_col, tokens, width)

    def y_copy(k):
        peer = lax.rem(me_c + k, n_col)
        return pltpu.make_async_remote_copy(
            src_ref=y_out.at[peer], dst_ref=y_in.at[me_c],
            send_sem=y_send.at[k], recv_sem=y_recv.at[k],
            device_id={"fsdp": peer}, device_id_type=MESH,
        )

    def y_start(k, carry):
        y_copy(k).start()
        return carry

    def y_wait(k, carry):
        peer = lax.rem(me_c - k + n_col, n_col)
        pltpu.make_async_remote_copy(
            src_ref=y_out.at[peer], dst_ref=y_in.at[peer],
            send_sem=y_send.at[k], recv_sem=y_recv.at[k],
            device_id={"fsdp": peer}, device_id_type=MESH,
        ).wait_recv()
        return carry

    lax.fori_loop(1, n_col, y_start, 0)
    y_in[me_c] = y_out[me_c]
    lax.fori_loop(1, n_col, y_wait, 0)
    out_ref[...] = y_in[...]

    for name in steps:
        for step, sends, _ in steps[name]:
            @pl.when(sends)
            def _():
                step.wait_send()
    for j in range(groups):
        def sent(k, carry):
            attn_copy(j, k).wait_send()
            return carry

        lax.fori_loop(1, n_col, sent, 0)

    def y_sent(k, carry):
        y_copy(k).wait_send()
        return carry

    lax.fori_loop(1, n_col, y_sent, 0)


def body(query, key_value, out_weight, mod_table, step, window):
    frames, rows, columns, features = query.shape
    heads = features // HEAD_DIM
    groups = heads // QUARTERS
    tokens = frames * rows * columns
    width = out_weight.shape[1]
    n_frame, n_row, n_col = (lax.axis_size(a) for a in ("frame", "row", "fsdp"))
    slots = frames + (1 if n_frame == 2 else 2)
    pairs = key_value.reshape(
        2, frames, rows // 2, 2, columns // 2, 2, QUARTERS, groups, HEAD_DIM)
    granules = pairs.transpose(1, 2, 4, 6, 3, 5, 7, 0, 8).reshape(
        frames, rows // 2, columns // 2, QUARTERS * 4, groups * 2 * HEAD_DIM)
    gate = lax.dynamic_slice(mod_table, (step[0], lax.axis_index("fsdp") * width), (1, width))
    block = (slots, rows // 2 + 2, columns // 2 + 2)
    keys = block[0] * block[1] * block[2] * 4
    vmem = pl.BlockSpec(memory_space=pltpu.VMEM)
    out = pl.pallas_call(
        functools.partial(kernel, (n_frame, n_row, n_col)),
        out_shape=jax.ShapeDtypeStruct((n_col, tokens, width), jnp.bfloat16),
        in_specs=[vmem, vmem, pl.BlockSpec(memory_space=pl.ANY), vmem,
                  pl.BlockSpec(memory_space=pltpu.SMEM)],
        out_specs=vmem,
        scratch_shapes=[
            pltpu.VMEM(block + granules.shape[3:], jnp.bfloat16),
            pltpu.VMEM((heads, tokens, keys), jnp.float32),
            pltpu.VMEM((groups, n_col, tokens, QUARTERS * HEAD_DIM), jnp.bfloat16),
            pltpu.VMEM(out_weight.shape, jnp.bfloat16),
            pltpu.VMEM((n_col, tokens, width), jnp.bfloat16),
            pltpu.VMEM((n_col, tokens, width), jnp.bfloat16),
            pltpu.SemaphoreType.DMA((12,)),
            pltpu.SemaphoreType.DMA((12,)),
            pltpu.SemaphoreType.DMA((groups, n_col)),
            pltpu.SemaphoreType.DMA((groups, n_col)),
            pltpu.SemaphoreType.DMA((n_col,)),
            pltpu.SemaphoreType.DMA((n_col,)),
            pltpu.SemaphoreType.DMA((2,)),
        ],
        compiler_params=pltpu.CompilerParams(
            collective_id=0, has_side_effects=True, vmem_limit_bytes=48 * 1024 * 1024),
    )(granules, query.reshape(tokens, features), out_weight, gate, window)
    mixed = out.transpose(1, 0, 2).reshape(tokens, n_col * width)
    return mixed.reshape(frames, rows, columns, -1)


def solution(mesh):
    return jax.shard_map(
        body,
        mesh=mesh,
        in_specs=(
            P("frame", "row", "fsdp", None),
            P(None, "frame", "row", "fsdp", None),
            P(None, "fsdp"),
            P(),
            P(),
            P(),
        ),
        out_specs=P("frame", "row", "fsdp", None),
        check_vma=False,
    )
```

time: 269 us -> 90.7 us (0.34)
  waiting for transfers between devices: 157 us -> 0 us
  Pallas kernels: 0 us -> 79.6 us
  local copies, waits for them, and re-layouts: 45.6 us -> 9.4 us
  starting transfers between devices: 18.4 us -> 0 us
  matrix products: 16.1 us -> 0 us
  other arithmetic: 15.9 us -> 0 us
  between operations: 14.3 us -> 0.74 us
    all_gather x1 -> x0, waiting for transfers between devices: 107 us -> none  [body(): lax.all_gather(out_weight, 'fsdp', axis=1, tiled=True)]
    pallas_call x0 -> x1, Pallas kernels: none -> 79.6 us  [body(): pl.pallas_call(functools.partial(kernel, (n_frame, n_row, n_col)), out_sh...]
    ppermute x6 -> x0, waiting for transfers between devices: 49.2 us -> none  [the longest x3 26 us: with_halo(): lax.ppermute(head, axis, [((i + 1) % count, i) for i in range(ends)])]
    ppermute x6 -> x0, starting transfers between devices: 18.4 us -> none  [the longest x3 13.7 us: with_halo(): lax.ppermute(tail, axis, [(i, (i + 1) % count) for i in range(ends)])]
    and x1 -> x0, local copies, waits for them, and re-layouts: 18 us -> none  [body(): frame_ok[:, :, None, None, :, None, None]]
    dot_general x3 -> x0, matrix products: 16.1 us -> none  [the longest x1 7.13 us: body(): jnp.dot(attn, lax.all_gather(out_weight, 'fsdp', axis=1, tiled=True), pre...]
    another operation x2, local copies, waits for them, and re-layouts: 9.72 us -> 1.36 us  [body(): return mixed.reshape(frames, rows, columns, -1)]
    and x8 -> x0, other arithmetic: 7.05 us -> none  [the longest x2 6.74 us: body(): frame_ok[:, :, None, None, :, None, None]]
  transfers between devices with their start and end apart: 7 -> 0, of which waited for: 6 -> 0; matrix products, arithmetic and copies ran while one was open for 25% -> 0% of each run, Pallas kernels for 0% -> 0%
where the time goes in v1:
time: 90.7 us; the launch traced here: 89.8 us
  Pallas kernels  79.6 us (88%)
  local copies, waits for them, and re-layouts  9.4 us (10%)
    pallas_call x1, Pallas kernels, body(): pl.pallas_call(functools.partial(kernel, (n_frame, n_row, n_col)), out_sh...  79.6 us
    reshape x1, local copies, waits for them, and re-layouts, body(): key_value.reshape(2, frames, rows // 2, 2, columns // 2, 2, QUARTERS, gro...  2.79 us
    unnamed x8, local copies, waits for them, and re-layouts  2.12 us

profile of v1, /device:TPU:1, one launch (start us, length us, event | category | flops | bytes accessed | tf_op | source)
XLA Modules:
  0.0 89.8 jit_solution(4014874596104600863)
XLA Ops:
  0.0 0.0 copy-start.1
  0.0 2.8 %reshape.9 = bf16[2,2,2,2,6,2,4,5,128]{8,7,6,3,2,5,4,1,0:T(8,128)(2,1)S(1)} reshape(bf16[2,2,4,12,2560]{4,2,3,1,0:T(4,128)(2,1)} %param.7) | data formatting | bytes 1966080 | tf_op jit(solution)/shard_map/reshape | solution.py:321
  2.8 0.0 copy-start.2
  2.8 1.5 %copy.10 = bf16[2,2,6,4,2,2,5,2,128]{8,7,6,5,4,3,2,1,0:T(2,128)(2,1)S(1)} copy(bf16[2,2,6,4,2,2,5,2,128]{8,6,3,4,1,5,2,0,7:T(8,128)(2,1)S(1)} %bitcast.9) | data formatting | bytes 1966080 | tf_op jit(solution)/shard_map/transpose | solution.py:323
  4.3 0.4 reshape.10.gin
  4.8 0.0 copy-done.1
  4.8 0.1 copy.11
  4.9 0.1 reshape.11.q_ref
  5.7 0.8 dynamic_slice.3.gate_ref
  6.5 0.0 copy-done.2
  6.5 0.1 copy.12.win_ref
  6.6 0.0 copy-start
  6.6 1.9 %copy-done = bf16[2560,640]{1,0:T(8,128)(2,1)S(1)} copy-done((bf16[2560,640]{1,0:T(8,128)(2,1)S(1)}, bf16[2560,640]{1,0:T(8,128)(2,1)}, u32[]{:S(2)}) %copy-start) | copy-done | bytes 3276824
  8.5 79.6 %shard_map.64 = bf16[4,96,640]{2,1,0:T(8,128)(2,1)S(1)} custom-call(bf16[2,2,6,16,1280]{4,3,2,1,0:T(8,128)(2,1)S(1)} %reshape.10.gin, bf16[96,2560]{1,0:T(8,128)(2,1)S(1)} %reshape.11.q_ref, bf16[2560,640]{1,0:T(8,128)(2,1)S(1)} %copy-done, f32[1,640]{1,0:T(1,128)S(1)} %dynamic_slice.3.gate_ref, s32[20,3]{1,0:T(8,128)S(1)} %copy.12.win_ref), custom_call_target="tpu_custom_call" | custom-call | tf_op jit(solution)/shard_map/pallas_call | solution.py:329
  88.1 0.3 copy.13
  88.4 0.2 reshape_reshape.3
  88.6 1.2 %copy.14 = bf16[2,4,12,2560]{3,1,2,0:T(4,128)(2,1)} copy(bf16[2,4,12,2560]{3,2,1,0:T(8,128)(2,1)S(1)} %reshape_reshape.3) | data formatting | bytes 983040 | tf_op jit(solution)/shard_map/reshape;reshape | solution.py:354
Async XLA Ops:
  0.0 4.8 %copy-start.1 = (bf16[2,4,12,2560]{3,1,2,0:T(4,128)(2,1)S(1)}, bf16[2,4,12,2560]{3,1,2,0:T(4,128)(2,1)}, u32[]{:S(2)}) copy-start(bf16[2,4,12,2560]{3,1,2,0:T(4,128)(2,1)} %param.6) | copy-start | bytes 1474564
  2.8 3.7 %copy-start.2 = (s32[20,3]{0,1:T(4,128)S(1)}, s32[20,3]{0,1:T(4,128)}, u32[]{:S(2)}) copy-start(s32[20,3]{0,1:T(4,128)} %param.11) | copy-start | bytes 724
  6.6 1.9 %copy-start = (bf16[2560,640]{1,0:T(8,128)(2,1)S(1)}, bf16[2560,640]{1,0:T(8,128)(2,1)}, u32[]{:S(2)}) copy-start(bf16[2560,640]{1,0:T(8,128)(2,1)} %w_hbm.1) | copy-start | bytes 9830404

commit v2 on v1

--- a/solution.py
+++ b/solution.py
@@ -10,18 +10,20 @@
 
 HEAD_DIM = 128
 QUARTERS = 4
+CHUNKS = ((0, 5),)
 MESH = pl.DeviceIdType.MESH
 
 
 def kernel(
     sizes, gin, q_ref, w_hbm, gate_ref, win_ref, out_ref,
-    grid, bias, attn, w_ref, y_out, y_in,
+    grid, bias, attn, w_ref, total, y_out, y_in,
     halo_send, halo_recv, attn_send, attn_recv, y_send, y_recv, local_sem,
 ):
     n_frame, n_row, n_col = sizes
     slots = grid.shape[0]
-    groups = attn.shape[0]
-    tokens = attn.shape[2]
+    groups = gin.shape[4] // (2 * HEAD_DIM)
+    tokens = q_ref.shape[0]
+    count = tokens // gin.shape[0]
     own_frames, own_rps, own_cps = gin.shape[:3]
     me_f = lax.axis_index("frame")
     me_r = lax.axis_index("row")
@@ -78,41 +80,52 @@
             (copy(down[0], down[1], index + 1, axis, me - 1), me > 0, me < count - 1),
         )
 
-    add("f", "frame", me_f, n_frame, 0,
-        (gin.at[own_frames - 1], grid.at[low_slot, own_r, own_c]),
-        (gin.at[0], grid.at[high_slot, own_r, own_c]))
-    add("r1", "row", me_r, n_row, 2,
-        (gin.at[:, own_rps - 1], grid.at[own_f, below, own_c]),
-        (gin.at[:, 0], grid.at[own_f, above, own_c]))
-    add("r2", "row", me_r, n_row, 4,
-        (grid.at[halo_f, own_rps - 1, own_c], grid.at[halo_f, below, own_c]),
-        (grid.at[halo_f, 0, own_c], grid.at[halo_f, above, own_c]))
-    add("c1", "fsdp", me_c, n_col, 6,
-        (gin.at[:, :, own_cps - 1], grid.at[own_f, own_r, left]),
-        (gin.at[:, :, 0], grid.at[own_f, own_r, right]))
-    add("c2", "fsdp", me_c, n_col, 8,
-        (grid.at[own_f, halo_r, own_cps - 1], grid.at[own_f, halo_r, left]),
-        (grid.at[own_f, halo_r, 0], grid.at[own_f, halo_r, right]))
+    every = slice(None)
     all_r = pl.ds(0, own_rps + 2)
-    add("c3", "fsdp", me_c, n_col, 10,
-        (grid.at[halo_f, all_r, own_cps - 1], grid.at[halo_f, all_r, left]),
-        (grid.at[halo_f, all_r, 0], grid.at[halo_f, all_r, right]))
-
-    def start(name):
-        for step, sends, _ in steps[name]:
+    for part, (low, high) in enumerate(CHUNKS):
+        base = 12 * part
+        tail = (every, pl.ds(low * 2 * HEAD_DIM, (high - low) * 2 * HEAD_DIM))
+
+        def own(*place):
+            return gin.at[place + tail]
+
+        def held(*place):
+            return grid.at[place + tail]
+
+        add(("f", part), "frame", me_f, n_frame, base,
+            (own(own_frames - 1, every, every), held(low_slot, own_r, own_c)),
+            (own(0, every, every), held(high_slot, own_r, own_c)))
+        add(("r1", part), "row", me_r, n_row, base + 2,
+            (own(every, own_rps - 1, every), held(own_f, below, own_c)),
+            (own(every, 0, every), held(own_f, above, own_c)))
+        add(("r2", part), "row", me_r, n_row, base + 4,
+            (held(halo_f, own_rps - 1, own_c), held(halo_f, below, own_c)),
+            (held(halo_f, 0, own_c), held(halo_f, above, own_c)))
+        add(("c1", part), "fsdp", me_c, n_col, base + 6,
+            (own(every, every, own_cps - 1), held(own_f, own_r, left)),
+            (own(every, every, 0), held(own_f, own_r, right)))
+        add(("c2", part), "fsdp", me_c, n_col, base + 8,
+            (held(own_f, halo_r, own_cps - 1), held(own_f, halo_r, left)),
+            (held(own_f, halo_r, 0), held(own_f, halo_r, right)))
+        add(("c3", part), "fsdp", me_c, n_col, base + 10,
+            (held(halo_f, all_r, own_cps - 1), held(halo_f, all_r, left)),
+            (held(halo_f, all_r, 0), held(halo_f, all_r, right)))
+
+    def start(name, part):
+        for step, sends, _ in steps[name, part]:
             @pl.when(sends)
             def _():
                 step.start()
 
-    def arrive(name):
-        for step, _, receives in steps[name]:
+    def arrive(name, part):
+        for step, _, receives in steps[name, part]:
             @pl.when(receives)
             def _():
                 step.wait_recv()
 
-    start("f")
-    start("r1")
-    start("c1")
+    start("f", 0)
+    start("r1", 0)
+    start("c1", 0)
 
     for edge, at_edge in (
         ((slice(None), below), me_r == 0),
@@ -136,8 +149,8 @@
                     grid[place, pair, pl.ds(0, own_cps)] = jnp.zeros(
                         (own_cps,) + grid.shape[3:], grid.dtype)
 
-    arrive("r1")
-    start("c2")
+    arrive("r1", 0)
+    start("c2", 0)
 
     keys = bias.shape[2]
     shape = (tokens, keys)
@@ -184,40 +197,64 @@
 
     lax.fori_loop(0, QUARTERS * groups, make_bias, 0)
 
-    arrive("f")
-    start("r2")
-    arrive("r2")
-    start("c3")
     own_copy.wait()
-    arrive("c1")
-    arrive("c2")
-    arrive("c3")
-
-    granules = slots * grid.shape[1] * grid.shape[2]
+    arrive("c1", 0)
+    arrive("c2", 0)
+
+    apart = n_frame == 2
+
+    def frame_at(turn):
+        if not apart:
+            return turn
+        return me_f if turn == 0 else own_frames - 1 - me_f
+
+    def frame_rows(turn):
+        return pl.ds(pl.multiple_of(frame_at(turn) * count, 16), count)
+
+    def relay(number):
+        if number == 0:
+            arrive("f", 0)
+            start("r2", 0)
+        else:
+            arrive("r2", 0)
+            start("c3", 0)
+
+    if not apart:
+        relay(0)
+        relay(1)
+        arrive("c3", 0)
+
+    pairs = grid.shape[1] * grid.shape[2]
     scale = 1.0 / math.sqrt(HEAD_DIM)
 
-    def attn_copy(j, k):
-        peer = lax.rem(me_c + k, n_col)
+    def block_copy(j, origin, way):
+        other = me_c + 1 - 2 * way
         return pltpu.make_async_remote_copy(
-            src_ref=attn.at[j, me_c], dst_ref=attn.at[j, me_c],
-            send_sem=attn_send.at[j, k], recv_sem=attn_recv.at[j, k],
-            device_id={"fsdp": peer}, device_id_type=MESH,
+            src_ref=attn.at[j, origin], dst_ref=attn.at[j, origin],
+            send_sem=attn_send.at[j, way, origin], recv_sem=attn_recv.at[j, origin],
+            device_id={"fsdp": other}, device_id_type=MESH,
         )
 
-    def attn_arrival(j, k):
-        peer = lax.rem(me_c - k + n_col, n_col)
-        return pltpu.make_async_remote_copy(
-            src_ref=attn.at[j, me_c], dst_ref=attn.at[j, peer],
-            send_sem=attn_send.at[j, k], recv_sem=attn_recv.at[j, k],
-            device_id={"fsdp": peer}, device_id_type=MESH,
-        )
-
-    for j in range(groups):
+    def wait_block(j, origin):
+        block_copy(j, origin, 0).wait_recv()
+
+    passes = (me_c < n_col - 1, me_c > 0)
+
+    def attend(turn):
+        used = own_frames if apart and turn == 0 else slots
+        for j in range(groups):
+            if apart and turn == 0 and j in (1, 3):
+                relay(j // 2)
+            attend_group(turn, j, used)
+
+    def attend_group(turn, j, used):
+        granules = used * pairs
+        length = granules * 4
+        rows = frame_rows(turn)
         lanes = pl.ds(j * 2 * HEAD_DIM, 2 * HEAD_DIM)
-        block = grid[:, :, :, :, lanes].astype(jnp.float32)
+        block = grid[pl.ds(0, used), :, :, :, lanes].astype(jnp.float32)
         block = block.reshape(granules // 2, 2, 2, 8, 2 * HEAD_DIM)
         first, second = block[:, 0], block[:, 1]
-        flat = (granules // 2 * 2 * 8, 2 * HEAD_DIM)
         turned_first = pltpu.roll(block[:, 0].reshape(-1, 8, 2 * HEAD_DIM), 4, 1).reshape(first.shape)
         turned_second = pltpu.roll(block[:, 1].reshape(-1, 8, 2 * HEAD_DIM), 4, 1).reshape(first.shape)
         upper = lax.broadcasted_iota(jnp.int32, first.shape, 2) < 4
@@ -225,89 +262,114 @@
         odd = jnp.where(upper, turned_first, second)
         for quarter in range(QUARTERS):
             head = quarter * groups + j
-            dense = (even, odd)[quarter % 2][:, quarter // 2].reshape(keys, 2 * HEAD_DIM)
+            dense = (even, odd)[quarter % 2][:, quarter // 2].reshape(length, 2 * HEAD_DIM)
             dense = dense.astype(jnp.bfloat16)
-            query = q_ref[:, pl.ds(head * HEAD_DIM, HEAD_DIM)]
+            query = q_ref[rows, pl.ds(head * HEAD_DIM, HEAD_DIM)]
             scores = lax.dot_general(
                 query, dense[:, :HEAD_DIM], (((1,), (1,)), ((), ())),
                 preferred_element_type=jnp.float32,
             )
-            scores = scores * scale + bias[head]
+            scores = scores * scale + bias[head, rows, pl.ds(0, length)]
             exponent = jnp.exp(scores - jnp.max(scores, axis=-1, keepdims=True))
             denominator = jnp.sum(exponent, axis=-1, keepdims=True)
             weights = (exponent * (1.0 / denominator)).astype(jnp.bfloat16)
             result = jnp.dot(weights, dense[:, HEAD_DIM:], preferred_element_type=jnp.float32)
-            attn[j, me_c, :, pl.ds(quarter * HEAD_DIM, HEAD_DIM)] = result.astype(jnp.bfloat16)
-
-        def send(k, carry):
-            attn_copy(j, k).start()
-            return carry
-
-        lax.fori_loop(1, n_col, send, 0)
-
-    w_copy.wait()
-    total = None
-    width = w_ref.shape[1]
-    for j in range(groups):
-        def gather(k, carry):
-            attn_arrival(j, k).wait_recv()
-            return carry
-
-        lax.fori_loop(1, n_col, gather, 0)
-        weight = jnp.concatenate(
-            [w_ref[pl.ds((quarter * groups + j) * HEAD_DIM, HEAD_DIM), :] for quarter in range(QUARTERS)],
-            axis=0,
-        )
-        part = jnp.dot(
-            attn[j].reshape(n_col * tokens, QUARTERS * HEAD_DIM), weight,
-            preferred_element_type=jnp.float32,
-        )
-        total = part if total is None else total + part
-    y_out[...] = (total * gate_ref[...]).astype(jnp.bfloat16).reshape(n_col, tokens, width)
-
-    def y_copy(k):
-        peer = lax.rem(me_c + k, n_col)
+            attn[turn * groups + j, me_c, :, pl.ds(quarter * HEAD_DIM, HEAD_DIM)] = result.astype(jnp.bfloat16)
+
+        for way in range(2):
+            @pl.when(passes[way])
+            def _():
+                block_copy(turn * groups + j, me_c, way).start()
+
+    def y_copy(turn, peer):
         return pltpu.make_async_remote_copy(
-            src_ref=y_out.at[peer], dst_ref=y_in.at[me_c],
-            send_sem=y_send.at[k], recv_sem=y_recv.at[k],
+            src_ref=y_out.at[turn, peer], dst_ref=y_in.at[turn, me_c],
+            send_sem=y_send.at[turn, peer], recv_sem=y_recv.at[turn, me_c],
             device_id={"fsdp": peer}, device_id_type=MESH,
         )
 
-    def y_start(k, carry):
-        y_copy(k).start()
+    def product(turn, j, origin):
+        weight = jnp.concatenate(
+            [w_ref[pl.ds((quarter * groups + j) * HEAD_DIM, HEAD_DIM), :]
+             for quarter in range(QUARTERS)], axis=0)
+        return jnp.dot(attn[turn * groups + j, origin], weight, preferred_element_type=jnp.float32)
+
+    def distance(turn, d, carry):
+        origins = (me_c - d, me_c + d)
+        there = (origins[0] >= 0, origins[1] < n_col)
+        for j in range(groups):
+            for way in range(2):
+                @pl.when(there[way])
+                def _():
+                    wait_block(turn * groups + j, origins[way])
+
+                    @pl.when(passes[way])
+                    def _():
+                        block_copy(turn * groups + j, origins[way], way).start()
+            for way in range(2):
+                @pl.when(there[way])
+                def _():
+                    part = product(turn, j, origins[way])
+                    if j > 0:
+                        part = total[way] + part
+                    if j < groups - 1:
+                        total[way] = part
+                    else:
+                        y_out[turn, origins[way]] = (part * gate_ref[...]).astype(jnp.bfloat16)
+                        y_copy(turn, origins[way]).start()
         return carry
 
-    def y_wait(k, carry):
-        peer = lax.rem(me_c - k + n_col, n_col)
-        pltpu.make_async_remote_copy(
-            src_ref=y_out.at[peer], dst_ref=y_in.at[peer],
-            send_sem=y_send.at[k], recv_sem=y_recv.at[k],
-            device_id={"fsdp": peer}, device_id_type=MESH,
-        ).wait_recv()
-        return carry
-
-    lax.fori_loop(1, n_col, y_start, 0)
-    y_in[me_c] = y_out[me_c]
-    lax.fori_loop(1, n_col, y_wait, 0)
-    out_ref[...] = y_in[...]
+    turns = own_frames
+    attend(0)
+    w_copy.wait()
+    distance(0, 1, 0)
+    if apart:
+        arrive("c3", 0)
+    for turn in range(1, turns):
+        attend(turn)
+    for turn in range(turns):
+        lax.fori_loop(2 if turn == 0 else 1, n_col, functools.partial(distance, turn), 0)
+    for turn in range(turns):
+        mine = product(turn, 0, me_c)
+        for j in range(1, groups):
+            mine += product(turn, j, me_c)
+        y_in[turn, me_c] = (mine * gate_ref[...]).astype(jnp.bfloat16)
+
+    for turn in range(turns):
+        def y_wait(k, carry):
+            peer = lax.rem(me_c + k, n_col)
+            pltpu.make_async_remote_copy(
+                src_ref=y_out.at[turn, peer], dst_ref=y_in.at[turn, peer],
+                send_sem=y_send.at[turn, peer], recv_sem=y_recv.at[turn, peer],
+                device_id={"fsdp": peer}, device_id_type=MESH,
+            ).wait_recv()
+            return carry
+
+        lax.fori_loop(1, n_col, y_wait, 0)
+        out_ref[:, frame_rows(turn), :] = y_in[turn]
 
     for name in steps:
         for step, sends, _ in steps[name]:
             @pl.when(sends)
             def _():
                 step.wait_send()
-    for j in range(groups):
-        def sent(k, carry):
-            attn_copy(j, k).wait_send()
+    for number in range(turns * groups):
+        for way in range(2):
+            def sent(d, carry):
+                origin = me_c - d + 2 * d * way
+
+                @pl.when(passes[way] & (origin >= 0) & (origin < n_col))
+                def _():
+                    block_copy(number, origin, way).wait_send()
+                return carry
+
+            lax.fori_loop(0, n_col, sent, 0)
+    for turn in range(turns):
+        def y_sent(k, carry):
+            y_copy(turn, lax.rem(me_c + k, n_col)).wait_send()
             return carry
 
-        lax.fori_loop(1, n_col, sent, 0)
-
-    def y_sent(k, carry):
-        y_copy(k).wait_send()
-        return carry
-
-    lax.fori_loop(1, n_col, y_sent, 0)
+        lax.fori_loop(1, n_col, y_sent, 0)
 
 
 def body(query, key_value, out_weight, mod_table, step, window):
@@ -335,20 +397,21 @@
         scratch_shapes=[
             pltpu.VMEM(block + granules.shape[3:], jnp.bfloat16),
             pltpu.VMEM((heads, tokens, keys), jnp.float32),
-            pltpu.VMEM((groups, n_col, tokens, QUARTERS * HEAD_DIM), jnp.bfloat16),
+            pltpu.VMEM((frames * groups, n_col, tokens // frames, QUARTERS * HEAD_DIM), jnp.bfloat16),
             pltpu.VMEM(out_weight.shape, jnp.bfloat16),
-            pltpu.VMEM((n_col, tokens, width), jnp.bfloat16),
-            pltpu.VMEM((n_col, tokens, width), jnp.bfloat16),
-            pltpu.SemaphoreType.DMA((12,)),
-            pltpu.SemaphoreType.DMA((12,)),
-            pltpu.SemaphoreType.DMA((groups, n_col)),
-            pltpu.SemaphoreType.DMA((groups, n_col)),
-            pltpu.SemaphoreType.DMA((n_col,)),
-            pltpu.SemaphoreType.DMA((n_col,)),
+            pltpu.VMEM((2, tokens // frames, width), jnp.float32),
+            pltpu.VMEM((frames, n_col, tokens // frames, width), jnp.bfloat16),
+            pltpu.VMEM((frames, n_col, tokens // frames, width), jnp.bfloat16),
+            pltpu.SemaphoreType.DMA((12 * len(CHUNKS),)),
+            pltpu.SemaphoreType.DMA((12 * len(CHUNKS),)),
+            pltpu.SemaphoreType.DMA((frames * groups, 2, n_col)),
+            pltpu.SemaphoreType.DMA((frames * groups, n_col)),
+            pltpu.SemaphoreType.DMA((frames, n_col)),
+            pltpu.SemaphoreType.DMA((frames, n_col)),
             pltpu.SemaphoreType.DMA((2,)),
         ],
         compiler_params=pltpu.CompilerParams(
-            collective_id=0, has_side_effects=True, vmem_limit_bytes=48 * 1024 * 1024),
+            collective_id=0, has_side_effects=True, vmem_limit_bytes=61 * 1024 * 1024),
     )(granules, query.reshape(tokens, features), out_weight, gate, window)
     mixed = out.transpose(1, 0, 2).reshape(tokens, n_col * width)
     return mixed.reshape(frames, rows, columns, -1)

time: 90.7 us -> 81.9 us (0.903)
  Pallas kernels: 79.6 us -> 69.5 us
  local copies, waits for them, and re-layouts: 9.4 us -> 11.4 us
    pallas_call x1, Pallas kernels: 79.6 us -> 69.5 us  [body(): pl.pallas_call(functools.partial(kernel, (n_frame, n_row, n_col)), out_sh...]
    unnamed x8 -> x6, local copies, waits for them, and re-layouts: 2.12 us -> 0.78 us
    transpose x1, local copies, waits for them, and re-layouts: 0.25 us -> 1.28 us  [body(): mixed = out.transpose(1, 0, 2).reshape(tokens, n_col * width)]
    reshape x1, local copies, waits for them, and re-layouts: 0.42 us -> 1.38 us  [body(): pairs.transpose(1, 2, 4, 6, 3, 5, 7, 0, 8)]
where the time goes in v2:
time: 81.9 us; the launch traced here: 81.6 us
  Pallas kernels  69.5 us (85%)
  local copies, waits for them, and re-layouts  11.4 us (14%)
    pallas_call x1, Pallas kernels, body(): pl.pallas_call(functools.partial(kernel, (n_frame, n_row, n_col)), out_sh...  69.5 us
    reshape x1, local copies, waits for them, and re-layouts, body(): key_value.reshape(2, frames, rows // 2, 2, columns // 2, 2, QUARTERS, gro...  2.79 us

profile of v2, /device:TPU:1, one launch (start us, length us, event | category | flops | bytes accessed | tf_op | source)
XLA Modules:
  0.0 81.6 jit_solution(6077452514399315996)
XLA Ops:
  0.0 0.0 copy-start
  0.0 2.8 %reshape.9 = bf16[2,2,2,2,6,2,4,5,128]{8,7,6,3,2,5,4,1,0:T(8,128)(2,1)S(1)} reshape(bf16[2,2,4,12,2560]{4,2,3,1,0:T(4,128)(2,1)} %param.7) | data formatting | bytes 1966080 | tf_op jit(solution)/shard_map/reshape | solution.py:383
  2.8 0.0 copy-start.1
  2.8 1.5 %copy.10 = bf16[2,2,6,4,2,2,5,2,128]{8,7,6,5,4,3,2,1,0:T(2,128)(2,1)S(1)} copy(bf16[2,2,6,4,2,2,5,2,128]{8,6,3,4,1,5,2,0,7:T(8,128)(2,1)S(1)} %bitcast.8) | data formatting | bytes 1966080 | tf_op jit(solution)/shard_map/transpose | solution.py:385
  4.3 1.4 %reshape.10.gin = bf16[2,2,6,16,1280]{4,3,2,1,0:T(8,128)(2,1)} reshape(bf16[2,2,6,4,2,2,5,2,128]{8,7,6,5,4,3,2,1,0:T(2,128)(2,1)S(1)} %copy.10) | data formatting | bytes 1966080 | tf_op jit(solution)/shard_map/reshape | solution.py:385
  5.7 0.0 copy-done
  5.7 0.1 copy.11
  5.8 0.9 %reshape.11.q_ref = bf16[96,2560]{1,0:T(8,128)(2,1)} reshape(bf16[2,4,12,2560]{3,2,1,0:T(8,128)(2,1)S(1)} %copy.11) | data formatting | bytes 983040 | tf_op jit(solution)/shard_map/reshape | solution.py:415
  7.4 1.4 %dynamic_slice.3.gate_ref = f32[1,640]{1,0:T(1,128)} dynamic-slice(f32[16,2560]{1,0:T(8,128)} %param.9, s32[]{:T(128)S(6)} %select_n.6, s32[]{:T(128)S(6)} %select_n.7), dynamic_slice_sizes={1,640} | dynamic-slice | bytes 5124 | tf_op jit(solution)/shard_map/dynamic_slice | solution.py:387
  8.8 0.0 copy-done.1
  8.8 0.7 copy.12.win_ref
  9.4 69.5 %shard_map.64 = bf16[4,96,640]{2,1,0:T(8,128)(2,1)} custom-call(bf16[2,2,6,16,1280]{4,3,2,1,0:T(8,128)(2,1)} %reshape.10.gin, bf16[96,2560]{1,0:T(8,128)(2,1)} %reshape.11.q_ref, bf16[2560,640]{1,0:T(8,128)(2,1)} %w_hbm.1, f32[1,640]{1,0:T(1,128)} %dynamic_slice.3.gate_ref, s32[20,3]{1,0:T(8,128)} %copy.12.win_ref), custom_call_target="tpu_custom_call" | custom-call | tf_op jit(solution)/shard_map/pallas_call | solution.py:391
  78.9 1.3 %copy.13 = bf16[96,4,640]{2,1,0:T(4,128)(2,1)S(1)} copy(bf16[96,4,640]{2,0,1:T(8,128)(2,1)} %bitcast.9) | data formatting | bytes 983040 | tf_op jit(solution)/shard_map/transpose | solution.py:416
  80.2 0.2 reshape_reshape.3
  80.4 1.2 %copy.14 = bf16[2,4,12,2560]{3,1,2,0:T(4,128)(2,1)} copy(bf16[2,4,12,2560]{3,2,1,0:T(8,128)(2,1)S(1)} %reshape_reshape.3) | data formatting | bytes 983040 | tf_op jit(solution)/shard_map/reshape;reshape | solution.py:417
Async XLA Ops:
  0.0 5.7 %copy-start = (bf16[2,4,12,2560]{3,1,2,0:T(4,128)(2,1)S(1)}, bf16[2,4,12,2560]{3,1,2,0:T(4,128)(2,1)}, u32[]{:S(2)}) copy-start(bf16[2,4,12,2560]{3,1,2,0:T(4,128)(2,1)} %param.6) | copy-start | bytes 1474564
  2.8 6.0 %copy-start.1 = (s32[20,3]{0,1:T(4,128)S(1)}, s32[20,3]{0,1:T(4,128)}, u32[]{:S(2)}) copy-start(s32[20,3]{0,1:T(4,128)} %param.11) | copy-start | bytes 724

commit v3 on v2

--- a/solution.py
+++ b/solution.py
@@ -15,7 +15,7 @@
 
 
 def kernel(
-    sizes, gin, q_ref, w_hbm, gate_ref, win_ref, out_ref,
+    sizes, gin, q_ref, w_hbm, mod_ref, step_ref, win_ref, out_ref,
     grid, bias, attn, w_ref, total, y_out, y_in,
     halo_send, halo_recv, attn_send, attn_recv, y_send, y_recv, local_sem,
 ):
@@ -191,7 +191,7 @@
     d_c = jnp.abs(k_c - q_c)
 
     def make_bias(head, carry):
-        ok = (d_f <= win_ref[head, 0]) & (d_r <= win_ref[head, 1]) & (d_c <= win_ref[head, 2])
+        ok = (d_f <= win_ref[0, head]) & (d_r <= win_ref[1, head]) & (d_c <= win_ref[2, head])
         bias[head] = jnp.where(ok, jnp.float32(0), jnp.float32(-1e30))
         return carry
 
@@ -315,10 +315,15 @@
                     if j < groups - 1:
                         total[way] = part
                     else:
-                        y_out[turn, origins[way]] = (part * gate_ref[...]).astype(jnp.bfloat16)
+                        y_out[turn, origins[way]] = (part * gate).astype(jnp.bfloat16)
                         y_copy(turn, origins[way]).start()
         return carry
 
+    width = w_ref.shape[1]
+    table_row = mod_ref[pl.ds(step_ref[0], 1), :]
+    gate = table_row[:, :width]
+    for place in range(1, n_col):
+        gate = jnp.where(me_c == place, table_row[:, place * width:(place + 1) * width], gate)
     turns = own_frames
     attend(0)
     w_copy.wait()
@@ -333,7 +338,7 @@
         mine = product(turn, 0, me_c)
         for j in range(1, groups):
             mine += product(turn, j, me_c)
-        y_in[turn, me_c] = (mine * gate_ref[...]).astype(jnp.bfloat16)
+        y_in[turn, me_c] = (mine * gate).astype(jnp.bfloat16)
 
     for turn in range(turns):
         def y_wait(k, carry):
@@ -384,7 +389,6 @@
         2, frames, rows // 2, 2, columns // 2, 2, QUARTERS, groups, HEAD_DIM)
     granules = pairs.transpose(1, 2, 4, 6, 3, 5, 7, 0, 8).reshape(
         frames, rows // 2, columns // 2, QUARTERS * 4, groups * 2 * HEAD_DIM)
-    gate = lax.dynamic_slice(mod_table, (step[0], lax.axis_index("fsdp") * width), (1, width))
     block = (slots, rows // 2 + 2, columns // 2 + 2)
     keys = block[0] * block[1] * block[2] * 4
     vmem = pl.BlockSpec(memory_space=pltpu.VMEM)
@@ -392,7 +396,7 @@
         functools.partial(kernel, (n_frame, n_row, n_col)),
         out_shape=jax.ShapeDtypeStruct((n_col, tokens, width), jnp.bfloat16),
         in_specs=[vmem, vmem, pl.BlockSpec(memory_space=pl.ANY), vmem,
-                  pl.BlockSpec(memory_space=pltpu.SMEM)],
+                  pl.BlockSpec(memory_space=pltpu.SMEM), pl.BlockSpec(memory_space=pltpu.SMEM)],
         out_specs=vmem,
         scratch_shapes=[
             pltpu.VMEM(block + granules.shape[3:], jnp.bfloat16),
@@ -411,8 +415,8 @@
             pltpu.SemaphoreType.DMA((2,)),
         ],
         compiler_params=pltpu.CompilerParams(
-            collective_id=0, has_side_effects=True, vmem_limit_bytes=61 * 1024 * 1024),
-    )(granules, query.reshape(tokens, features), out_weight, gate, window)
+            collective_id=0, has_side_effects=True, vmem_limit_bytes=40 * 1024 * 1024),
+    )(granules, query.reshape(tokens, features), out_weight, mod_table, step, window.T)
     mixed = out.transpose(1, 0, 2).reshape(tokens, n_col * width)
     return mixed.reshape(frames, rows, columns, -1)
 

time: 81.9 us -> 77.7 us (0.949)
  local copies, waits for them, and re-layouts: 11.4 us -> 8.49 us
  Pallas kernels: 69.5 us -> 68.3 us
    dynamic_slice x1 -> x0, local copies, waits for them, and re-layouts: 1.39 us -> none  [body(): lax.dynamic_slice(mod_table, (step[0], lax.axis_index('fsdp') * width), (...]
    unnamed x6 -> x9, local copies, waits for them, and re-layouts: 0.78 us -> 2.03 us
    pallas_call x1, Pallas kernels: 69.5 us -> 68.3 us  [body(): pl.pallas_call(functools.partial(kernel, (n_frame, n_row, n_col)), out_sh...]
    transpose x1, local copies, waits for them, and re-layouts: 1.28 us -> 0.25 us  [body(): mixed = out.transpose(1, 0, 2).reshape(tokens, n_col * width)]
    reshape x1, local copies, waits for them, and re-layouts: 1.38 us -> 0.42 us  [body(): pairs.transpose(1, 2, 4, 6, 3, 5, 7, 0, 8)]
where the time goes in v3:
time: 77.7 us; the launch traced here: 77.5 us
  Pallas kernels  68.3 us (88%)
  local copies, waits for them, and re-layouts  8.49 us (11%)
    pallas_call x1, Pallas kernels, body(): pl.pallas_call(functools.partial(kernel, (n_frame, n_row, n_col)), out_sh...  68.3 us
    reshape x1, local copies, waits for them, and re-layouts, body(): key_value.reshape(2, frames, rows // 2, 2, columns // 2, 2, QUARTERS, gro...  2.79 us
    unnamed x9, local copies, waits for them, and re-layouts  2.03 us

profile of v3, /device:TPU:1, one launch (start us, length us, event | category | flops | bytes accessed | tf_op | source)
XLA Modules:
  0.0 77.5 jit_solution(10730030929220475026)
XLA Ops:
  0.0 0.0 copy-start.3
  0.0 2.8 %reshape.9 = bf16[2,2,2,2,6,2,4,5,128]{8,7,6,3,2,5,4,1,0:T(8,128)(2,1)S(1)} reshape(bf16[2,2,4,12,2560]{4,2,3,1,0:T(4,128)(2,1)} %param.7) | data formatting | bytes 1966080 | tf_op jit(solution)/shard_map/reshape | solution.py:388
  2.8 0.0 copy-start.1
  2.8 0.0 copy-start.2
  2.8 1.5 %copy.9 = bf16[2,2,6,4,2,2,5,2,128]{8,7,6,5,4,3,2,1,0:T(2,128)(2,1)S(1)} copy(bf16[2,2,6,4,2,2,5,2,128]{8,6,3,4,1,5,2,0,7:T(8,128)(2,1)S(1)} %bitcast.7) | data formatting | bytes 1966080 | tf_op jit(solution)/shard_map/transpose | solution.py:390
  4.4 0.4 reshape.10.gin
  4.8 0.0 copy-done.3
  4.8 0.1 copy.10
  4.9 0.1 reshape.11.q_ref
  5.7 0.0 copy-done.1
  5.7 0.0 copy-done.2
  5.7 0.0 copy-start
  5.7 1.9 %copy-done = bf16[2560,640]{1,0:T(8,128)(2,1)S(1)} copy-done((bf16[2560,640]{1,0:T(8,128)(2,1)S(1)}, bf16[2560,640]{1,0:T(8,128)(2,1)}, u32[]{:S(2)}) %copy-start) | copy-done | bytes 3276824
  7.6 68.3 %shard_map.64 = bf16[4,96,640]{2,1,0:T(8,128)(2,1)S(1)} custom-call(bf16[2,2,6,16,1280]{4,3,2,1,0:T(8,128)(2,1)S(1)} %reshape.10.gin, bf16[96,2560]{1,0:T(8,128)(2,1)S(1)} %reshape.11.q_ref, bf16[2560,640]{1,0:T(8,128)(2,1)S(1)} %copy-done, f32[16,2560]{1,0:T(8,128)S(1)} %copy-done.1, s32[1]{0:T(128)S(6)} %copy.13.step_ref, s32[3,20]{1,0:T(4,128)S(1)} %bitcast.6), custom_call_target="tpu_custom_call" | custom-call | tf_op jit(solution)/shard_map/pallas_call | solution.py:395
  75.9 0.3 copy.11
  76.1 0.2 reshape_reshape.3
  76.3 1.2 %copy.12 = bf16[2,4,12,2560]{3,1,2,0:T(4,128)(2,1)} copy(bf16[2,4,12,2560]{3,2,1,0:T(8,128)(2,1)S(1)} %reshape_reshape.3) | data formatting | bytes 983040 | tf_op jit(solution)/shard_map/reshape;reshape | solution.py:421
Async XLA Ops:
  0.0 4.8 %copy-start.3 = (bf16[2,4,12,2560]{3,1,2,0:T(4,128)(2,1)S(1)}, bf16[2,4,12,2560]{3,1,2,0:T(4,128)(2,1)}, u32[]{:S(2)}) copy-start(bf16[2,4,12,2560]{3,1,2,0:T(4,128)(2,1)} %param.6) | copy-start | bytes 1474564
  2.8 2.9 %copy-start.1 = (f32[16,2560]{1,0:T(8,128)S(1)}, f32[16,2560]{1,0:T(8,128)}, u32[]{:S(2)}) copy-start(f32[16,2560]{1,0:T(8,128)} %mod_ref.1) | copy-start | bytes 491524
  2.8 2.9 %copy-start.2 = (s32[20,3]{0,1:T(4,128)S(1)}, s32[20,3]{0,1:T(4,128)}, u32[]{:S(2)}) copy-start(s32[20,3]{0,1:T(4,128)} %param.11) | copy-start | bytes 724
  5.7 1.9 %copy-start = (bf16[2560,640]{1,0:T(8,128)(2,1)S(1)}, bf16[2560,640]{1,0:T(8,128)(2,1)}, u32[]{:S(2)}) copy-start(bf16[2560,640]{1,0:T(8,128)(2,1)} %w_hbm.1) | copy-start | bytes 9830404

commit v4 on v3

--- a/solution.py
+++ b/solution.py
@@ -351,7 +351,8 @@
             return carry
 
         lax.fori_loop(1, n_col, y_wait, 0)
-        out_ref[:, frame_rows(turn), :] = y_in[turn]
+        for place in range(n_col):
+            out_ref[frame_rows(turn), place * width:(place + 1) * width] = y_in[turn, place]
 
     for name in steps:
         for step, sends, _ in steps[name]:
@@ -394,7 +395,7 @@
     vmem = pl.BlockSpec(memory_space=pltpu.VMEM)
     out = pl.pallas_call(
         functools.partial(kernel, (n_frame, n_row, n_col)),
-        out_shape=jax.ShapeDtypeStruct((n_col, tokens, width), jnp.bfloat16),
+        out_shape=jax.ShapeDtypeStruct((tokens, n_col * width), jnp.bfloat16),
         in_specs=[vmem, vmem, pl.BlockSpec(memory_space=pl.ANY), vmem,
                   pl.BlockSpec(memory_space=pltpu.SMEM), pl.BlockSpec(memory_space=pltpu.SMEM)],
         out_specs=vmem,
@@ -417,8 +418,7 @@
         compiler_params=pltpu.CompilerParams(
             collective_id=0, has_side_effects=True, vmem_limit_bytes=40 * 1024 * 1024),
     )(granules, query.reshape(tokens, features), out_weight, mod_table, step, window.T)
-    mixed = out.transpose(1, 0, 2).reshape(tokens, n_col * width)
-    return mixed.reshape(frames, rows, columns, -1)
+    return out.reshape(frames, rows, columns, -1)
 
 
 def solution(mesh):

time: 77.7 us -> 77.3 us (level)
    another operation x2 -> x0, local copies, waits for them, and re-layouts: 1.36 us -> none  [body(): return mixed.reshape(frames, rows, columns, -1)]
    reshape x0 -> x2, local copies, waits for them, and re-layouts: none -> 1.27 us  [body(): return out.reshape(frames, rows, columns, -1)]
where the time goes in v4:
time: 77.3 us; the launch traced here: 77.1 us
  Pallas kernels  68.3 us (88%)
  local copies, waits for them, and re-layouts  8.15 us (11%)
    pallas_call x1, Pallas kernels, body(): pl.pallas_call(functools.partial(kernel, (n_frame, n_row, n_col)), out_sh...  68.3 us
    reshape x1, local copies, waits for them, and re-layouts, body(): key_value.reshape(2, frames, rows // 2, 2, columns // 2, 2, QUARTERS, gro...  2.79 us
    unnamed x9, local copies, waits for them, and re-layouts  2.03 us

profile of v4, /device:TPU:1, one launch (start us, length us, event | category | flops | bytes accessed | tf_op | source)
XLA Modules:
  0.0 77.1 jit_solution(214983646761091115)
XLA Ops:
  0.0 0.0 copy-start.3
  0.0 2.8 %reshape.12 = bf16[2,2,2,2,6,2,4,5,128]{8,7,6,3,2,5,4,1,0:T(8,128)(2,1)S(1)} reshape(bf16[2,2,4,12,2560]{4,2,3,1,0:T(4,128)(2,1)} %param.7) | data formatting | bytes 1966080 | tf_op jit(solution)/shard_map/reshape | solution.py:389
  2.8 0.0 copy-start.1
  2.8 0.0 copy-start.2
  2.8 1.5 %copy.10 = bf16[2,2,6,4,2,2,5,2,128]{8,7,6,5,4,3,2,1,0:T(2,128)(2,1)S(1)} copy(bf16[2,2,6,4,2,2,5,2,128]{8,6,3,4,1,5,2,0,7:T(8,128)(2,1)S(1)} %bitcast.5) | data formatting | bytes 1966080 | tf_op jit(solution)/shard_map/transpose | solution.py:391
  4.4 0.4 reshape.13.gin
  4.8 0.0 copy-done.3
  4.8 0.1 copy.11
  4.9 0.1 reshape.14.q_ref
  5.7 0.0 copy-done.1
  5.7 0.0 copy-done.2
  5.7 0.0 copy-start
  5.7 1.9 %copy-done = bf16[2560,640]{1,0:T(8,128)(2,1)S(1)} copy-done((bf16[2560,640]{1,0:T(8,128)(2,1)S(1)}, bf16[2560,640]{1,0:T(8,128)(2,1)}, u32[]{:S(2)}) %copy-start) | copy-done | bytes 3276824
  7.6 68.3 %shard_map.64 = bf16[96,2560]{1,0:T(8,128)(2,1)S(1)} custom-call(bf16[2,2,6,16,1280]{4,3,2,1,0:T(8,128)(2,1)S(1)} %reshape.13.gin, bf16[96,2560]{1,0:T(8,128)(2,1)S(1)} %reshape.14.q_ref, bf16[2560,640]{1,0:T(8,128)(2,1)S(1)} %copy-done, f32[16,2560]{1,0:T(8,128)S(1)} %copy-done.1, s32[1]{0:T(128)S(6)} %copy.13.step_ref, s32[3,20]{1,0:T(4,128)S(1)} %bitcast.4), custom_call_target="tpu_custom_call" | custom-call | tf_op jit(solution)/shard_map/pallas_call | solution.py:396
  75.9 0.1 reshape.15
  76.0 1.2 %copy.12 = bf16[2,4,12,2560]{3,1,2,0:T(4,128)(2,1)} copy(bf16[2,4,12,2560]{3,2,1,0:T(8,128)(2,1)S(1)} %reshape.15) | data formatting | bytes 983040 | tf_op jit(solution)/shard_map/reshape | solution.py:421
Async XLA Ops:
  0.0 4.8 %copy-start.3 = (bf16[2,4,12,2560]{3,1,2,0:T(4,128)(2,1)S(1)}, bf16[2,4,12,2560]{3,1,2,0:T(4,128)(2,1)}, u32[]{:S(2)}) copy-start(bf16[2,4,12,2560]{3,1,2,0:T(4,128)(2,1)} %param.6) | copy-start | bytes 1474564
  2.8 2.9 %copy-start.1 = (f32[16,2560]{1,0:T(8,128)S(1)}, f32[16,2560]{1,0:T(8,128)}, u32[]{:S(2)}) copy-start(f32[16,2560]{1,0:T(8,128)} %mod_ref.1) | copy-start | bytes 491524
  2.8 2.9 %copy-start.2 = (s32[20,3]{0,1:T(4,128)S(1)}, s32[20,3]{0,1:T(4,128)}, u32[]{:S(2)}) copy-start(s32[20,3]{0,1:T(4,128)} %param.11) | copy-start | bytes 724
  5.7 1.9 %copy-start = (bf16[2560,640]{1,0:T(8,128)(2,1)S(1)}, bf16[2560,640]{1,0:T(8,128)(2,1)}, u32[]{:S(2)}) copy-start(bf16[2560,640]{1,0:T(8,128)(2,1)} %w_hbm.1) | copy-start | bytes 9830404
